TPU v7x, 32 devices: a whole 2x2x4 slice. The times are simulated.
32 devices in a mesh: patch: 8 (over y, x, core), tensor: 4 (over z).
Axes of the slice: x: 2, y: 2, z: 4, core: 2. Of those that a mesh axis runs over, the one named last changes fastest.
Arguments:
- query: bfloat16 [4096, 5120], P('patch', 'tensor'), may hold values from -6 to 6
- key_fresh: bfloat16 [4096, 5120], P('patch', 'tensor'), may hold values from -6 to 6
- value_fresh: bfloat16 [4096, 5120], P('patch', 'tensor'), may hold values from -6 to 6
- key_stale: bfloat16 [4096, 5120], P('patch', 'tensor'), may hold values from -6 to 6
- value_stale: bfloat16 [4096, 5120], P('patch', 'tensor'), may hold values from -6 to 6
- out_weight: bfloat16 [5120, 5120], P('tensor'), may hold values from -0.078125 to 0.078125
- residual: bfloat16 [4096, 5120], P('patch', 'tensor'), may hold values from -6 to 6
- gate: float32 [5120], P('tensor'), may hold values from 0.5 to 1.5
Outputs:
- block_out: bfloat16 [4096, 5120], P('patch', 'tensor')
All inputs are finite; a program needn't handle non-finite values.
Results may differ from a plain program's by a relative error of at most 0.006.
Values may be sent and summed in bfloat16 or wider, within the bound.
A program may use at most 128 MiB of HBM per device.

v0:
```python
import functools
import math

import jax
import jax.numpy as jnp
from jax import lax
from jax.experimental import pallas as pl
from jax.experimental.pallas import tpu as pltpu
from jax.sharding import PartitionSpec as P

HD = 128
SCALE = HD ** -0.5 * math.log2(math.e)


def attend_block(q, k, v, m_old, acc_old):
    s = lax.dot_general(q, k, (((1,), (1,)), ((), ())), preferred_element_type=jnp.float32) * SCALE
    m_new = jnp.maximum(m_old, jnp.max(s, axis=-1, keepdims=True))
    p = jnp.exp2(s - m_new).astype(jnp.bfloat16)
    v1 = jnp.concatenate([v, jnp.ones_like(v)], axis=1)
    add = jnp.dot(p, v1, preferred_element_type=jnp.float32)
    return m_new, acc_old * jnp.exp2(m_old - m_new) + add


def flash_kernel(n, q_ref, kf_ref, vf_ref, ks_ref, vs_ref, o_ref):
    rows = q_ref.shape[0]
    own = lax.axis_index("patch")
    q = q_ref[...]
    m0 = jnp.full((rows, 1), -1e30, jnp.float32)
    a0 = jnp.zeros((rows, 2 * HD), jnp.float32)
    state = attend_block(q, kf_ref[...], vf_ref[...], m0, a0)

    def inner(j, state):
        first = pl.multiple_of(lax.rem(own + j, n) * rows, rows)
        return attend_block(q, ks_ref[pl.ds(first, rows), :], vs_ref[pl.ds(first, rows), :], *state)

    m, acc = lax.fori_loop(1, n, inner, state)
    o_ref[...] = (acc[:, :HD] / acc[:, HD:]).astype(o_ref.dtype)


def general_body(n, query, key_fresh, value_fresh, key_stale, value_stale, out_weight, residual, gate):
    rows, cols = query.shape
    keys = lax.all_gather(key_stale, "patch", axis=0, tiled=True)
    values = lax.all_gather(value_stale, "patch", axis=0, tiled=True)
    local = pl.BlockSpec((rows, HD), lambda h: (0, h))
    whole = pl.BlockSpec((rows * n, HD), lambda h: (0, h))
    attended = pl.pallas_call(
        functools.partial(flash_kernel, n),
        grid=(cols // HD,),
        in_specs=[local, local, local, whole, whole],
        out_specs=local,
        out_shape=jax.ShapeDtypeStruct((rows, cols), jnp.bfloat16),
        compiler_params=pltpu.CompilerParams(vmem_limit_bytes=48 * 2**20),
        name="flash",
    )(query, key_fresh, value_fresh, keys, values)
    partial = jnp.dot(attended, out_weight, preferred_element_type=jnp.float32).astype(jnp.bfloat16)
    mine = lax.psum_scatter(partial, "tensor", scatter_dimension=1, tiled=True).astype(jnp.float32)
    return (residual.astype(jnp.float32) + gate[None, :] * mine).astype(jnp.bfloat16)


def solution(mesh):
    n = mesh.shape["patch"]
    both = P("patch", "tensor")
    return jax.shard_map(
        functools.partial(general_body, n),
        mesh=mesh,
        in_specs=(both,) * 5 + (P("tensor", None), both, P("tensor")),
        out_specs=both,
        check_vma=False,
    )
```

profile of v0, /device:TPU:8, one launch (start us, length us, event | category | flops | bytes accessed | tf_op | source)
XLA Modules:
  0.0 329.5 jit_solution(16613090246223773524)
XLA Ops:
  6.5 0.0 copy-start.1
  6.5 0.0 copy-start
  6.5 0.0 all-gather.3.cloned.1.call-start
  6.5 0.7 all-gather.3.cloned.1.call-update
  7.3 0.0 all-gather.5.cloned.1.call-start
  7.3 0.7 all-gather.5.cloned.1.call-update
  8.0 0.0 reduce-scatter.2.cloned.1.call-start
  8.1 65.6 %all-gather.3.cloned.1.call-done.ks_ref = bf16[4096,1280]{1,0:T(8,128)(2,1)} async-done(((bf16[512,1280]{1,0:T(8,128)(2,1)}), bf16[4096,1280]{1,0:T(8,128)(2,1)}) %all-gather.3.cloned.1.call-update) | async-done | bytes 10485776 | tf_op jit(solution)/shard_map/all_gather | solution.py:42
  73.7 65.2 %all-gather.5.cloned.1.call-done.vs_ref = bf16[4096,1280]{1,0:T(8,128)(2,1)} async-done(((bf16[512,1280]{1,0:T(8,128)(2,1)}), bf16[4096,1280]{1,0:T(8,128)(2,1)}) %all-gather.5.cloned.1.call-update) | async-done | bytes 10485776 | tf_op jit(solution)/shard_map/all_gather | solution.py:43
  138.9 0.0 copy-done.1
  138.9 0.0 copy-done
  138.9 0.0 copy-start.2
  138.9 1.3 copy-done.2
  140.2 72.7 %flash.1 = bf16[512,1280]{1,0:T(8,128)(2,1)S(1)} custom-call(bf16[512,1280]{1,0:T(8,128)(2,1)S(1)} %copy-done, bf16[512,1280]{1,0:T(8,128)(2,1)S(1)} %copy-done.1, bf16[512,1280]{1,0:T(8,128)(2,1)S(1)} %copy-done.2, bf16[4096,1280]{1,0:T(8,128)(2,1)} %all-gather.3.cloned.1.call-done.ks_ref, bf16[4096,1280]{1,0:T(8,128)(2,1)} %all-gather.5.cloned.1.call-done.vs_ref), custom_call_target="tpu_custom_call" | custom-call | tf_op jit(solution)/shard_map/flash/pallas_call | solution.py:46
  212.9 13.4 %convolution_convert_fusion = bf16[512,5120]{1,0:T(8,128)(2,1)} fusion(bf16[512,1280]{1,0:T(8,128)(2,1)S(1)} %flash.1, bf16[1280,5120]{1,0:T(8,128)(2,1)} %param.13), kind=kOutput, calls=%fused_computation | convolution fusion | flops 6713507840 | bytes 19660800 | tf_op jit(solution)/shard_map/dot_general | solution.py:55
  226.3 0.0 copy-start.3
  226.3 0.0 copy-start.4
  226.3 0.0 reduce-scatter.2.cloned.1.call-update
  226.3 93.9 %reduce-scatter.2.cloned.1.call-done = bf16[512,1280]{1,0:T(8,128)(2,1)} async-done(((bf16[512,5120]{1,0:T(8,128)(2,1)}), bf16[512,1280]{1,0:T(8,128)(2,1)}) %reduce-scatter.2.cloned.1.call-update) | async-done | bytes 1310736 | tf_op jit(solution)/shard_map/reduce_scatter | solution.py:56
  320.3 0.0 copy-done.3
  320.3 0.0 copy-done.4
  320.3 2.8 add_convert_fusion
Async XLA Ops:
  6.5 132.3 %copy-start.1 = (bf16[512,1280]{1,0:T(8,128)(2,1)S(1)}, bf16[512,1280]{1,0:T(8,128)(2,1)}, u32[]{:S(2)}) copy-start(bf16[512,1280]{1,0:T(8,128)(2,1)} %kf_ref.1) | copy-start | bytes 3932164
  6.5 132.3 %copy-start = (bf16[512,1280]{1,0:T(8,128)(2,1)S(1)}, bf16[512,1280]{1,0:T(8,128)(2,1)}, u32[]{:S(2)}) copy-start(bf16[512,1280]{1,0:T(8,128)(2,1)} %q_ref.1) | copy-start | bytes 3932164
  6.5 67.2 %all-gather.3.cloned.1.call-start = ((), (), s32[]{:S(2)}) async-start(), calls=%async_computation.1 | async-start | bytes 11796480 | tf_op jit(solution)/shard_map/all_gather | solution.py:42
  7.3 131.6 %all-gather.5.cloned.1.call-start = ((), (), s32[]{:S(2)}) async-start(), calls=%async_computation.2 | async-start | bytes 11796480 | tf_op jit(solution)/shard_map/all_gather | solution.py:43
  8.0 312.2 %reduce-scatter.2.cloned.1.call-start = ((), (), s32[]{:S(2)}) async-start(), calls=%async_computation.3 | async-start | bytes 6553600 | tf_op jit(solution)/shard_map/reduce_scatter | solution.py:56
  138.9 1.3 copy-start.2
  226.3 93.9 %copy-start.3 = (bf16[512,1280]{1,0:T(8,128)(2,1)S(1)}, bf16[512,1280]{1,0:T(8,128)(2,1)}, u32[]{:S(2)}) copy-start(bf16[512,1280]{1,0:T(8,128)(2,1)} %param.14) | copy-start | bytes 3932164
  226.3 93.9 %copy-start.4 = (f32[1280]{0:T(1024)S(1)}, f32[1280]{0:T(1024)}, u32[]{:S(2)}) copy-start(f32[1280]{0:T(1024)} %param.15) | copy-start | bytes 15364
Sparse Core Ops, SparseCore 0:
  9.2 64.4 all-gather.2
  75.6 63.2 all-gather.4
  226.5 93.7 reduce-scatter.1
where the time goes:
time: 331 us; the launch traced here: 330 us
  waiting for transfers between devices  226 us (68%)
  Pallas kernels  72.7 us (22%)
  matrix products  13.4 us (4%)
  between operations  13.1 us (4%)
    reduce_scatter x1, waiting for transfers between devices, general_body(): lax.psum_scatter(partial, 'tensor', scatter_dimension=1, tiled=True)  93.9 us
    pallas_call x1, Pallas kernels, general_body(): pl.pallas_call(functools.partial(flash_kernel, n), grid=(cols // HD,), in...  72.7 us
    all_gather x1, waiting for transfers between devices, general_body(): keys = lax.all_gather(key_stale, 'patch', axis=0, tiled=True)  65.6 us
    all_gather x1, waiting for transfers between devices, general_body(): values = lax.all_gather(value_stale, 'patch', axis=0, tiled=True)  65.2 us
    dot_general x1, matrix products, general_body(): jnp.dot(attended, out_weight, preferred_element_type=jnp.float32)  13.4 us
  transfers between devices with their start and end apart: 3, of which 3 were waited for; matrix products, arithmetic and copies ran while one was open for 0% of the time, Pallas kernels for 0%

commit v1 on v0

--- a/solution.py
+++ b/solution.py
@@ -37,8 +37,203 @@
     o_ref[...] = (acc[:, :HD] / acc[:, HD:]).astype(o_ref.dtype)
 
 
+MESH = pl.DeviceIdType.MESH
+
+
+def attend_kernel(q_ref, kf_ref, vf_ref, ks_ref, vs_ref, o_ref, kv, qx, osend, orecv, lsend, lrecv,
+                  m_s, acc_s, first_s, first_q, fwd_s, ret_s, rec_kv, rec_q, rec_o):
+    own = lax.axis_index("patch")
+    c, x, y = lax.rem(own, 2), lax.rem(own // 2, 2), own // 4
+
+    def at(ky, kx, kc):
+        return lax.rem(y + ky, 2) * 4 + lax.rem(x + kx, 2) * 2 + lax.rem(c + kc, 2)
+
+    pc, px, py, pyx = at(0, 0, 1), at(0, 1, 0), at(1, 0, 0), at(1, 1, 0)
+    half = kv.shape[0]
+    rows = q_ref.shape[0]
+
+    def head_cols(hx, i):
+        return pl.ds(pl.multiple_of((hx * half + i) * HD, HD), HD)
+
+    def send(src, dst, ssem, rsem, dev):
+        return pltpu.make_async_remote_copy(src_ref=src, dst_ref=dst, send_sem=ssem, recv_sem=rsem,
+                                            device_id={"patch": dev}, device_id_type=MESH)
+
+    def firsts(i):
+        mine, theirs = head_cols(x, i), head_cols(1 - x, i)
+        out = [send(q_ref.at[:, theirs], qx.at[i], first_q.at[i], rec_q.at[i], px)]
+        for t, src in enumerate((ks_ref, vs_ref)):
+            out.append(send(src.at[:, theirs], kv.at[i, own, t], first_s.at[0, i, t], rec_kv.at[i, own], px))
+            out.append(send(src.at[:, mine], kv.at[i, own, t], first_s.at[1, i, t], rec_kv.at[i, own], py))
+            out.append(send(src.at[:, mine], kv.at[i, own, t], first_s.at[2, i, t], rec_kv.at[i, own], pc))
+            out.append(pltpu.make_async_copy(src.at[:, mine], kv.at[i, own, t], first_s.at[3, i, t]))
+        return out
+
+    def start_first(i):
+        for copy in firsts(i):
+            copy.start()
+
+    def fwd(kind, i, b, dev):
+        return send(kv.at[i, b], kv.at[i, b], fwd_s.at[kind, i], rec_kv.at[i, b], dev)
+
+    def arrived(i, b):
+        fwd(0, i, b, pc).wait_recv()
+
+    def back(i):
+        return (send(osend.at[i], orecv.at[i], ret_s.at[0, i], rec_o.at[0, i], px),
+                send(lsend.at[i], lrecv.at[i], ret_s.at[1, i], rec_o.at[1, i], px))
+
+    def pass_on_x(i):
+        arrived(i, px)
+        fwd(0, i, px, py).start()
+        fwd(1, i, px, pc).start()
+
+    def fold(i, q, blocks):
+        for r in range(2):
+            m, acc = attend_block(q[r], kv[i, blocks[r], 0], kv[i, blocks[r], 1], m_s[r], acc_s[r])
+            m_s[r], acc_s[r] = m, acc
+
+    def merge(i):
+        theirs = head_cols(1 - x, i)
+        for copy in back(i):
+            copy.wait_recv()
+        m = jnp.broadcast_to(lrecv[i][0:1, :], (HD, rows)).T[:, 0:1]
+        acc = jnp.concatenate([orecv[i].astype(jnp.float32), jnp.ones((rows, HD), jnp.float32)], axis=1)
+        m, acc = attend_block(q_ref[:, theirs], kf_ref[:, theirs], vf_ref[:, theirs], m, acc)
+        o_ref[:, theirs] = (acc[:, :HD] / acc[:, HD:]).astype(o_ref.dtype)
+
+    barrier = pltpu.get_barrier_semaphore()
+    for dev in (pc, px, py):
+        pl.semaphore_signal(barrier, inc=1, device_id={"patch": dev}, device_id_type=MESH)
+    pl.semaphore_wait(barrier, 3)
+
+    start_first(0)
+    start_first(1)
+
+    def one_head(i, _):
+        @pl.when(i + 2 < half)
+        def _():
+            start_first(i + 2)
+
+        mine = head_cols(x, i)
+        m0 = jnp.full((rows, 1), -1e30, jnp.float32)
+        a0 = jnp.zeros((rows, 2 * HD), jnp.float32)
+        m_s[0], acc_s[0] = attend_block(q_ref[:, mine], kf_ref[:, mine], vf_ref[:, mine], m0, a0)
+        m_s[1], acc_s[1] = m0, a0
+
+        @pl.when(i == 0)
+        def _():
+            pass_on_x(0)
+
+        send(q_ref.at[:, mine], qx.at[i], first_q.at[i], rec_q.at[i], px).wait_recv()
+        for t, src in enumerate((ks_ref, vs_ref)):
+            pltpu.make_async_copy(src.at[:, mine], kv.at[i, own, t], first_s.at[3, i, t]).wait()
+        arrived(i, pc)
+        arrived(i, at(0, 1, 1))
+
+        def queries():
+            return q_ref[:, mine], qx[i]
+
+        def near(t, _):
+            kx, kc = (t + 1) // 2, lax.rem(t + 1, 2)
+            b0 = at(0, kx, kc)
+            b1 = lax.rem(t, 2) * own + (1 - lax.rem(t, 2)) * b0
+            fold(i, queries(), (b0, b1))
+            return 0
+
+        lax.fori_loop(0, 3, near, 0)
+
+        @pl.when(i + 1 < half)
+        def _():
+            pass_on_x(i + 1)
+
+        arrived(i, py)
+        fwd(2, i, py, pc).start()
+        arrived(i, pyx)
+        fwd(3, i, pyx, pc).start()
+
+        def far(t, _):
+            @pl.when(t == 2)
+            def _():
+                arrived(i, at(1, 0, 1))
+                arrived(i, at(1, 1, 1))
+
+            b = at(1, lax.rem(t, 2), t // 2)
+            fold(i, queries(), (b, b))
+            return 0
+
+        lax.fori_loop(0, 4, far, 0)
+        o_ref[:, mine] = (acc_s[0][:, :HD] / acc_s[0][:, HD:]).astype(o_ref.dtype)
+        total = acc_s[1][:, HD:]
+        osend[i] = (acc_s[1][:, :HD] / total).astype(osend.dtype)
+        lsend[i] = (m_s[1] + jnp.log2(total)).T[0:8, :]
+        for copy in back(i):
+            copy.start()
+
+        @pl.when(i > 0)
+        def _():
+            merge(i - 1)
+
+        return 0
+
+    lax.fori_loop(0, half, one_head, 0)
+    merge(half - 1)
+
+    def finish(i, _):
+        firsts_i = firsts(i)
+        firsts_i[0].wait_send()
+        for t in range(2):
+            for k in range(3):
+                firsts_i[1 + 4 * t + k].wait_send()
+        for kind, (b, dev) in enumerate(((px, py), (px, pc), (py, pc), (pyx, pc))):
+            fwd(kind, i, b, dev).wait_send()
+        for copy in back(i):
+            copy.wait_send()
+        return 0
+
+    lax.fori_loop(0, half, finish, 0)
+
+
+def paired_attention(query, key_fresh, value_fresh, key_stale, value_stale):
+    rows, cols = query.shape
+    half = cols // HD // 2
+    vmem = pl.BlockSpec(memory_space=pltpu.VMEM)
+    hbm = pl.BlockSpec(memory_space=pl.ANY)
+    dma = pltpu.SemaphoreType.DMA
+    bf16, f32 = jnp.bfloat16, jnp.float32
+    return pl.pallas_call(
+        attend_kernel,
+        in_specs=[vmem, vmem, vmem, hbm, hbm],
+        out_specs=vmem,
+        out_shape=jax.ShapeDtypeStruct((rows, cols), bf16),
+        scratch_shapes=[
+            pltpu.VMEM((half, 8, 2, rows, HD), bf16),
+            pltpu.VMEM((half, rows, HD), bf16),
+            pltpu.VMEM((half, rows, HD), bf16),
+            pltpu.VMEM((half, rows, HD), bf16),
+            pltpu.VMEM((half, 8, rows), f32),
+            pltpu.VMEM((half, 8, rows), f32),
+            pltpu.VMEM((2, rows, 1), f32),
+            pltpu.VMEM((2, rows, 2 * HD), f32),
+            dma((4, half, 2)),
+            dma((half,)),
+            dma((4, half)),
+            dma((2, half)),
+            dma((half, 8)),
+            dma((half,)),
+            dma((2, half)),
+        ],
+        compiler_params=pltpu.CompilerParams(
+            collective_id=1, has_side_effects=True, vmem_limit_bytes=56 * 2**20
+        ),
+        name="paired_attention",
+    )(query, key_fresh, value_fresh, key_stale, value_stale)
+
 def general_body(n, query, key_fresh, value_fresh, key_stale, value_stale, out_weight, residual, gate):
     rows, cols = query.shape
+    if n == 8 and cols % (2 * HD) == 0:
+        attended = paired_attention(query, key_fresh, value_fresh, key_stale, value_stale)
+        return project(attended, out_weight, residual, gate)
     keys = lax.all_gather(key_stale, "patch", axis=0, tiled=True)
     values = lax.all_gather(value_stale, "patch", axis=0, tiled=True)
     local = pl.BlockSpec((rows, HD), lambda h: (0, h))
@@ -52,6 +247,10 @@
         compiler_params=pltpu.CompilerParams(vmem_limit_bytes=48 * 2**20),
         name="flash",
     )(query, key_fresh, value_fresh, keys, values)
+    return project(attended, out_weight, residual, gate)
+
+
+def project(attended, out_weight, residual, gate):
     partial = jnp.dot(attended, out_weight, preferred_element_type=jnp.float32).astype(jnp.bfloat16)
     mine = lax.psum_scatter(partial, "tensor", scatter_dimension=1, tiled=True).astype(jnp.float32)
     return (residual.astype(jnp.float32) + gate[None, :] * mine).astype(jnp.bfloat16)

time: 331 us -> 220 us (0.66)
  waiting for transfers between devices: 226 us -> 94.2 us
  Pallas kernels: 72.7 us -> 94.3 us
    all_gather x2 -> x0, waiting for transfers between devices: 131 us -> none  [the longest x1 65.6 us: general_body(): keys = lax.all_gather(key_stale, 'patch', axis=0, tiled=True)]
    pallas_call x1, Pallas kernels: 72.7 us -> 94.3 us  [paired_attention(): pl.pallas_call(attend_kernel, in_specs=[vmem, vmem, vmem, hbm, hbm], out_...]
  transfers between devices with their start and end apart: 3 -> 1, of which waited for: 3 -> 1; matrix products, arithmetic and copies ran while one was open for 0% -> 0% of each run, Pallas kernels for 0% -> 0%
where the time goes in v1:
time: 220 us; the launch traced here: 218 us
  Pallas kernels  94.3 us (43%)
  waiting for transfers between devices  94.2 us (43%)
  matrix products  13.6 us (6%)
  between operations  13.4 us (6%)
  other arithmetic  2.76 us (1%)
    pallas_call x1, Pallas kernels, paired_attention(): pl.pallas_call(attend_kernel, in_specs=[vmem, vmem, vmem, hbm, hbm], out_...  94.3 us
    reduce_scatter x1, waiting for transfers between devices, project(): lax.psum_scatter(partial, 'tensor', scatter_dimension=1, tiled=True)  94.2 us
    dot_general x1, matrix products, project(): jnp.dot(attended, out_weight, preferred_element_type=jnp.float32)  13.6 us
  transfers between devices with their start and end apart: 1, of which 1 were waited for; matrix products, arithmetic and copies ran while one was open for 0% of the time, Pallas kernels for 0%

profile of v1, /device:TPU:8, one launch (start us, length us, event | category | flops | bytes accessed | tf_op | source)
XLA Modules:
  0.0 218.3 jit_solution(16667434759631124707)
XLA Ops:
  6.5 0.0 reduce-scatter.2.cloned.1.call-start
  6.5 94.3 %paired_attention.1 = bf16[512,1280]{1,0:T(8,128)(2,1)} custom-call(bf16[512,1280]{1,0:T(8,128)(2,1)} %q_ref.1, bf16[512,1280]{1,0:T(8,128)(2,1)} %kf_ref.1, bf16[512,1280]{1,0:T(8,128)(2,1)} %vf_ref.1, bf16[512,1280]{1,0:T(8,128)(2,1)} %ks_ref.1, bf16[512,1280]{1,0:T(8,128)(2,1)} %vs_ref.1), custom_call_target="tpu_custom_call" | custom-call | tf_op jit(solution)/shard_map/paired_attention/pallas_call | solution.py:204
  100.9 13.6 %convolution_convert_fusion = bf16[512,5120]{1,0:T(8,128)(2,1)} fusion(bf16[512,1280]{1,0:T(8,128)(2,1)} %paired_attention.1, bf16[1280,5120]{1,0:T(8,128)(2,1)} %param.13), kind=kOutput, calls=%fused_computation | convolution fusion | flops 6713507840 | bytes 19660800 | tf_op jit(solution)/shard_map/dot_general | solution.py:254
  114.5 0.0 copy-start
  114.5 0.0 copy-start.1
  114.5 0.0 reduce-scatter.2.cloned.1.call-update
  114.5 94.2 %reduce-scatter.2.cloned.1.call-done = bf16[512,1280]{1,0:T(8,128)(2,1)} async-done(((bf16[512,5120]{1,0:T(8,128)(2,1)}), bf16[512,1280]{1,0:T(8,128)(2,1)}) %reduce-scatter.2.cloned.1.call-update) | async-done | bytes 1310736 | tf_op jit(solution)/shard_map/reduce_scatter | solution.py:255
  208.7 0.0 copy-done
  208.7 0.0 copy-done.1
  208.7 2.8 %add_convert_fusion = bf16[512,1280]{1,0:T(8,128)(2,1)} fusion(bf16[512,1280]{1,0:T(8,128)(2,1)} %reduce-scatter.2.cloned.1.call-done, bf16[512,1280]{1,0:T(8,128)(2,1)S(1)} %copy-done, f32[1280]{0:T(1024)S(1)} %copy-done.1), kind=kLoop, calls=%fused_computation.1 | loop fusion | flops 3276800 | bytes 3937280 | tf_op jit(solution)/shard_map/convert_element_type | solution.py:256
Async XLA Ops:
  6.5 202.2 %reduce-scatter.2.cloned.1.call-start = ((), (), s32[]{:S(2)}) async-start(), calls=%async_computation.1 | async-start | bytes 6553600 | tf_op jit(solution)/shard_map/reduce_scatter | solution.py:255
  114.5 94.2 %copy-start = (bf16[512,1280]{1,0:T(8,128)(2,1)S(1)}, bf16[512,1280]{1,0:T(8,128)(2,1)}, u32[]{:S(2)}) copy-start(bf16[512,1280]{1,0:T(8,128)(2,1)} %param.14) | copy-start | bytes 3932164
  114.5 94.2 %copy-start.1 = (f32[1280]{0:T(1024)S(1)}, f32[1280]{0:T(1024)}, u32[]{:S(2)}) copy-start(f32[1280]{0:T(1024)} %param.15) | copy-start | bytes 15364
Sparse Core Ops, SparseCore 0:
  114.6 94.0 reduce-scatter.1

commit v2 on v1

--- a/solution.py
+++ b/solution.py
@@ -40,8 +40,8 @@
 MESH = pl.DeviceIdType.MESH
 
 
-def attend_kernel(q_ref, kf_ref, vf_ref, ks_ref, vs_ref, o_ref, kv, qx, osend, orecv, lsend, lrecv,
-                  m_s, acc_s, first_s, first_q, fwd_s, ret_s, rec_kv, rec_q, rec_o):
+def attend_kernel(q_ref, kf_ref, vf_ref, ks_ref, vs_ref, w_ref, o_ref, wx_ref, kv, qx, osend, orecv, lsend, lrecv,
+                  m_s, acc_s, first_s, first_q, fwd_s, ret_s, rec_kv, rec_q, rec_o, w_s, rec_w):
     own = lax.axis_index("patch")
     c, x, y = lax.rem(own, 2), lax.rem(own // 2, 2), own // 4
 
@@ -51,6 +51,10 @@
     pc, px, py, pyx = at(0, 0, 1), at(0, 1, 0), at(1, 0, 0), at(1, 1, 0)
     half = kv.shape[0]
     rows = q_ref.shape[0]
+    z = lax.axis_index("tensor")
+    mate = z + 1 - 2 * lax.rem(z, 2)
+    outer = lax.rem(z, 3) == 0
+    width = wx_ref.shape[1]
 
     def head_cols(hx, i):
         return pl.ds(pl.multiple_of((hx * half + i) * HD, HD), HD)
@@ -69,9 +73,32 @@
             out.append(pltpu.make_async_copy(src.at[:, mine], kv.at[i, own, t], first_s.at[3, i, t]))
         return out
 
+    def weight_rows(core, i):
+        return pl.ds(pl.multiple_of((core * half + i) * HD, HD), HD)
+
+    def weight_out(i):
+        cols = pl.ds(pl.multiple_of((1 - z // 2) * width, HD), width)
+        return pltpu.make_async_remote_copy(
+            src_ref=w_ref.at[weight_rows(c, i), cols], dst_ref=wx_ref.at[weight_rows(c, i), :],
+            send_sem=w_s.at[i], recv_sem=rec_w.at[0, i], device_id={"tensor": mate}, device_id_type=MESH)
+
+    def weight_on(i, core):
+        part = wx_ref.at[weight_rows(core, i), :]
+        return send(part, part, w_s.at[i], rec_w.at[1, i], pc)
+
+    def weight_pass(i):
+        @pl.when(jnp.logical_not(outer))
+        def _():
+            weight_out(i).wait_recv()
+            weight_on(i, c).start()
+
     def start_first(i):
         for copy in firsts(i):
             copy.start()
+
+        @pl.when(outer)
+        def _():
+            weight_out(i).start()
 
     def fwd(kind, i, b, dev):
         return send(kv.at[i, b], kv.at[i, b], fwd_s.at[kind, i], rec_kv.at[i, b], dev)
@@ -105,7 +132,8 @@
     barrier = pltpu.get_barrier_semaphore()
     for dev in (pc, px, py):
         pl.semaphore_signal(barrier, inc=1, device_id={"patch": dev}, device_id_type=MESH)
-    pl.semaphore_wait(barrier, 3)
+    pl.semaphore_signal(barrier, inc=1, device_id={"tensor": mate}, device_id_type=MESH)
+    pl.semaphore_wait(barrier, 4)
 
     start_first(0)
     start_first(1)
@@ -173,13 +201,24 @@
         @pl.when(i > 0)
         def _():
             merge(i - 1)
+            weight_pass(i - 1)
 
         return 0
 
     lax.fori_loop(0, half, one_head, 0)
     merge(half - 1)
+    weight_pass(half - 1)
 
     def finish(i, _):
+        @pl.when(outer)
+        def _():
+            weight_out(i).wait_send()
+
+        @pl.when(jnp.logical_not(outer))
+        def _():
+            weight_on(i, c).wait_send()
+            weight_on(i, 1 - c).wait_recv()
+
         firsts_i = firsts(i)
         firsts_i[0].wait_send()
         for t in range(2):
@@ -194,7 +233,7 @@
     lax.fori_loop(0, half, finish, 0)
 
 
-def paired_attention(query, key_fresh, value_fresh, key_stale, value_stale):
+def paired_attention(query, key_fresh, value_fresh, key_stale, value_stale, out_weight):
     rows, cols = query.shape
     half = cols // HD // 2
     vmem = pl.BlockSpec(memory_space=pltpu.VMEM)
@@ -203,9 +242,10 @@
     bf16, f32 = jnp.bfloat16, jnp.float32
     return pl.pallas_call(
         attend_kernel,
-        in_specs=[vmem, vmem, vmem, hbm, hbm],
-        out_specs=vmem,
-        out_shape=jax.ShapeDtypeStruct((rows, cols), bf16),
+        in_specs=[vmem, vmem, vmem, hbm, hbm, hbm],
+        out_specs=[vmem, hbm],
+        out_shape=[jax.ShapeDtypeStruct((rows, cols), bf16),
+                   jax.ShapeDtypeStruct((cols, out_weight.shape[1] // 2), bf16)],
         scratch_shapes=[
             pltpu.VMEM((half, 8, 2, rows, HD), bf16),
             pltpu.VMEM((half, rows, HD), bf16),
@@ -222,18 +262,193 @@
             dma((half, 8)),
             dma((half,)),
             dma((2, half)),
+            dma((half,)),
+            dma((2, half)),
         ],
         compiler_params=pltpu.CompilerParams(
             collective_id=1, has_side_effects=True, vmem_limit_bytes=56 * 2**20
         ),
         name="paired_attention",
-    )(query, key_fresh, value_fresh, key_stale, value_stale)
+    )(query, key_fresh, value_fresh, key_stale, value_stale, out_weight)
+
+
+def project_kernel(a_ref, w_ref, wx_ref, res_ref, gate_ref, o_ref, w, wx, am, pm, sfo, spe, f, tfo, tpe,
+                   fs, ps, own_s, w_s, send_s, rec_s):
+    z = lax.axis_index("tensor")
+    mate = z + 1 - 2 * lax.rem(z, 2)
+    outer = lax.rem(z, 3) == 0
+    inner = jnp.logical_not(outer)
+    peer = 3 - z
+    far = 2 * (1 - z // 2)
+    jfo, jpe = lax.rem(z, 2), 1 - lax.rem(z, 2)
+    chunks, step, share = am.shape
+
+    def load(s):
+        cols = pl.ds(pl.multiple_of(s * share, HD), share)
+        return pltpu.make_async_copy(w_ref.at[:, cols], w.at[s], w_s.at[s])
+
+    def load_x(j):
+        cols = pl.ds(pl.multiple_of(j * share, HD), share)
+        return pltpu.make_async_copy(wx_ref.at[:, cols], wx.at[j], w_s.at[4 + j])
+
+    def rows_of(r):
+        return pl.ds(pl.multiple_of(r * step, step), step)
+
+    def send(kind, src, dst, r, dev):
+        return pltpu.make_async_remote_copy(src_ref=src, dst_ref=dst.at[r], send_sem=send_s.at[kind, r],
+                                            recv_sem=rec_s.at[kind, r], device_id={"tensor": dev},
+                                            device_id_type=MESH)
+
+    def c_att(r):
+        return send(0, a_ref.at[rows_of(r), :], am, r, mate)
+
+    def c_part(r):
+        return send(1, ps.at[r], pm, r, mate)
+
+    def c_fo(r):
+        return send(2, tfo.at[r], sfo, r, peer)
+
+    def c_pe(r):
+        return send(3, tpe.at[r], spe, r, peer)
+
+    def c_fin(r):
+        return send(4, fs.at[r], f, r, mate)
+
+    def dot(lhs, rhs):
+        return jnp.dot(lhs, rhs, preferred_element_type=jnp.float32)
+
+    def mine(r):
+        return a_ref[rows_of(r), :]
+
+    def each(fn):
+        def one(r, _):
+            fn(r)
+            return 0
+
+        lax.fori_loop(0, chunks, one, 0)
+
+    def store(r, total):
+        o_ref[rows_of(r), :] = (
+            res_ref[rows_of(r), :].astype(jnp.float32) + gate_ref[...] * total
+        ).astype(o_ref.dtype)
+
+    barrier = pltpu.get_barrier_semaphore()
+    pl.semaphore_signal(barrier, inc=1, device_id={"tensor": mate}, device_id_type=MESH)
+
+    @pl.when(inner)
+    def _():
+        pl.semaphore_signal(barrier, inc=1, device_id={"tensor": peer}, device_id_type=MESH)
+        pl.semaphore_wait(barrier, 2)
+        order = (load(far + jfo), load_x(jfo), load(far + jpe), load_x(jpe), load(mate), load(z))
+        for copy in order:
+            copy.start()
+        for copy in order[:2]:
+            copy.wait()
+
+        @each
+        def _(r):
+            c_att(r).wait_recv()
+            tfo[r] = (dot(mine(r), w[far + jfo]) + dot(am[r], wx[jfo])).astype(jnp.bfloat16)
+            c_fo(r).start()
+
+        for copy in order[2:]:
+            copy.wait()
+
+        @each
+        def _(r):
+            tpe[r] = (dot(mine(r), w[far + jpe]) + dot(am[r], wx[jpe])).astype(jnp.bfloat16)
+            c_pe(r).start()
+            own_s[r] = dot(mine(r), w[mate])
+            c_fo(r).wait_recv()
+            fs[r] = (own_s[r] + sfo[r].astype(jnp.float32)).astype(jnp.bfloat16)
+            c_fin(r).start()
+
+        @each
+        def _(r):
+            own_s[r] = dot(mine(r), w[z])
+
+        @each
+        def _(r):
+            c_part(r).wait_recv()
+            c_pe(r).wait_recv()
+            store(r, own_s[r] + pm[r].astype(jnp.float32) + spe[r].astype(jnp.float32))
+
+        @each
+        def _(r):
+            c_fo(r).wait_send()
+            c_pe(r).wait_send()
+            c_fin(r).wait_send()
+
+    @pl.when(outer)
+    def _():
+        pl.semaphore_wait(barrier, 1)
+
+        @each
+        def _(r):
+            c_att(r).start()
+
+        order = (load(mate), load(z))
+        for copy in order:
+            copy.start()
+        for copy in order:
+            copy.wait()
+
+        @each
+        def _(r):
+            ps[r] = dot(mine(r), w[mate]).astype(jnp.bfloat16)
+            c_part(r).start()
+            own_s[r] = dot(mine(r), w[z])
+
+        @each
+        def _(r):
+            c_fin(r).wait_recv()
+            store(r, own_s[r] + f[r].astype(jnp.float32))
+
+        @each
+        def _(r):
+            c_att(r).wait_send()
+            c_part(r).wait_send()
+
+
+def line_project(attended, weight_mate, out_weight, residual, gate):
+    rows, cols = attended.shape
+    share = out_weight.shape[1] // 4
+    chunks = rows // 128
+    vmem = pl.BlockSpec(memory_space=pltpu.VMEM)
+    hbm = pl.BlockSpec(memory_space=pl.ANY)
+    dma = pltpu.SemaphoreType.DMA
+    bf16, f32 = jnp.bfloat16, jnp.float32
+    blocks = [pltpu.VMEM((chunks, 128, share), bf16) for _ in range(7)]
+    return pl.pallas_call(
+        project_kernel,
+        in_specs=[vmem, hbm, hbm, vmem, vmem],
+        out_specs=vmem,
+        out_shape=jax.ShapeDtypeStruct((rows, share), bf16),
+        scratch_shapes=[
+            pltpu.VMEM((4, cols, share), bf16),
+            pltpu.VMEM((2, cols, share), bf16),
+            pltpu.VMEM((chunks, 128, cols), bf16),
+            *blocks,
+            pltpu.VMEM((chunks, 128, share), bf16),
+            pltpu.VMEM((chunks, 128, share), f32),
+            dma((6,)),
+            dma((5, chunks)),
+            dma((5, chunks)),
+        ],
+        compiler_params=pltpu.CompilerParams(
+            collective_id=2, has_side_effects=True, vmem_limit_bytes=56 * 2**20
+        ),
+        name="line_project",
+    )(attended, out_weight, weight_mate, residual, gate[None, :])
+
 
 def general_body(n, query, key_fresh, value_fresh, key_stale, value_stale, out_weight, residual, gate):
     rows, cols = query.shape
-    if n == 8 and cols % (2 * HD) == 0:
-        attended = paired_attention(query, key_fresh, value_fresh, key_stale, value_stale)
-        return project(attended, out_weight, residual, gate)
+    if n == 8 and lax.axis_size("tensor") == 4 and cols % (2 * HD) == 0:
+        attended, weight_mate = paired_attention(
+            query, key_fresh, value_fresh, key_stale, value_stale, out_weight
+        )
+        return line_project(attended, weight_mate, out_weight, residual, gate)
     keys = lax.all_gather(key_stale, "patch", axis=0, tiled=True)
     values = lax.all_gather(value_stale, "patch", axis=0, tiled=True)
     local = pl.BlockSpec((rows, HD), lambda h: (0, h))

time: 220 us -> 174 us (0.79)
  waiting for transfers between devices: 94.2 us -> 0 us
  Pallas kernels: 94.3 us -> 170 us
  matrix products: 13.6 us -> 0 us
  between operations: 13.4 us -> 0.02 us
  local copies, waits for them, and re-layouts: 0.01 us -> 3.75 us
  other arithmetic: 2.76 us -> 0 us
    reduce_scatter x1 -> x0, waiting for transfers between devices: 94.2 us -> none  [project(): lax.psum_scatter(partial, 'tensor', scatter_dimension=1, tiled=True)]
    pallas_call x1 -> x2, Pallas kernels: 94.3 us -> 170 us  [the longest x1 96.4 us: paired_attention(): pl.pallas_call(attend_kernel, in_specs=[vmem, vmem, vmem, hbm, hbm, hbm],...]
    dot_general x1 -> x0, matrix products: 13.6 us -> none  [project(): jnp.dot(attended, out_weight, preferred_element_type=jnp.float32)]
    convert_element_type x1 -> x0, other arithmetic: 2.76 us -> none  [project(): (residual.astype(jnp.float32) + gate[None, :] * mine).astype(jnp.bfloat16)]
    unnamed x4 -> x1, local copies, waits for them, and re-layouts: 0.01 us -> 2.46 us
  transfers between devices with their start and end apart: 1 -> 0, of which waited for: 1 -> 0; matrix products, arithmetic and copies ran while one was open for 0% -> 0% of each run, Pallas kernels for 0% -> 0%
where the time goes in v2:
time: 174 us
  Pallas kernels  170 us (98%)
  local copies, waits for them, and re-layouts  3.75 us (2%)
    pallas_call x1, Pallas kernels, paired_attention(): pl.pallas_call(attend_kernel, in_specs=[vmem, vmem, vmem, hbm, hbm, hbm],...  96.4 us
    pallas_call x1, Pallas kernels, line_project(): pl.pallas_call(project_kernel, in_specs=[vmem, hbm, hbm, vmem, vmem], out...  73.8 us

profile of v2, /device:TPU:8, one launch (start us, length us, event | category | flops | bytes accessed | tf_op | source)
XLA Modules:
  0.0 174.0 jit_solution(16277318203780637169)
XLA Ops:
  0.0 1.3 broadcast_in_dim.3.gate_ref
  1.3 96.4 %paired_attention.1 = (bf16[512,1280]{1,0:T(8,128)(2,1)}, bf16[1280,2560]{1,0:T(8,128)(2,1)}) custom-call(bf16[512,1280]{1,0:T(8,128)(2,1)} %q_ref.1, bf16[512,1280]{1,0:T(8,128)(2,1)} %kf_ref.1, bf16[512,1280]{1,0:T(8,128)(2,1)} %vf_ref.1, bf16[512,1280]{1,0:T(8,128)(2,1)} %ks_ref.1, bf16[512,1280]{1,0:T(8,128)(2,1)} %vs_ref.1, bf16[1280,5120]{1,0:T(8,128)(2,1)} %w_ref.3), custom_call_target="tpu_custom_call" | custom-call | tf_op jit(solution)/shard_map/paired_attention/pallas_call | solution.py:243
  97.8 73.8 %line_project.1 = bf16[512,1280]{1,0:T(8,128)(2,1)} custom-call(bf16[512,1280]{1,0:T(8,128)(2,1)} %get-tuple-element.7.a_ref, bf16[1280,5120]{1,0:T(8,128)(2,1)} %w_ref.3, bf16[1280,2560]{1,0:T(8,128)(2,1)} %get-tuple-element.8.wx_ref, bf16[512,1280]{1,0:T(8,128)(2,1)} %res_ref.1, f32[1,1280]{1,0:T(1,128)} %broadcast_in_dim.3.gate_ref), custom_call_target="tpu_custom_call" | custom-call | tf_op jit(solution)/shard_map/line_project/pallas_call | solution.py:422
  171.5 2.5 %copy.10 = bf16[512,1280]{1,0:T(8,128)(2,1)} copy(bf16[512,1280]{1,0:T(8,128)(2,1)} %line_project.1) | data formatting | bytes 2621440

commit v3 on v2

--- a/solution.py
+++ b/solution.py
@@ -15,17 +15,17 @@
 def attend_block(q, k, v, m_old, acc_old):
     s = lax.dot_general(q, k, (((1,), (1,)), ((), ())), preferred_element_type=jnp.float32) * SCALE
     m_new = jnp.maximum(m_old, jnp.max(s, axis=-1, keepdims=True))
-    p = jnp.exp2(s - m_new).astype(jnp.bfloat16)
+    p = jnp.exp2(s - jnp.tile(m_new, (1, s.shape[1] // HD))).astype(jnp.bfloat16)
     v1 = jnp.concatenate([v, jnp.ones_like(v)], axis=1)
     add = jnp.dot(p, v1, preferred_element_type=jnp.float32)
-    return m_new, acc_old * jnp.exp2(m_old - m_new) + add
+    return m_new, acc_old * jnp.tile(jnp.exp2(m_old - m_new), (1, 2)) + add
 
 
 def flash_kernel(n, q_ref, kf_ref, vf_ref, ks_ref, vs_ref, o_ref):
     rows = q_ref.shape[0]
     own = lax.axis_index("patch")
     q = q_ref[...]
-    m0 = jnp.full((rows, 1), -1e30, jnp.float32)
+    m0 = jnp.full((rows, HD), -1e30, jnp.float32)
     a0 = jnp.zeros((rows, 2 * HD), jnp.float32)
     state = attend_block(q, kf_ref[...], vf_ref[...], m0, a0)
 
@@ -38,6 +38,7 @@
 
 
 MESH = pl.DeviceIdType.MESH
+FRESH, PX, PC, PXC, OWN, PY, PYX, PYC, PYXC = range(9)
 
 
 def attend_kernel(q_ref, kf_ref, vf_ref, ks_ref, vs_ref, w_ref, o_ref, wx_ref, kv, qx, osend, orecv, lsend, lrecv,
@@ -48,9 +49,10 @@
     def at(ky, kx, kc):
         return lax.rem(y + ky, 2) * 4 + lax.rem(x + kx, 2) * 2 + lax.rem(c + kc, 2)
 
-    pc, px, py, pyx = at(0, 0, 1), at(0, 1, 0), at(1, 0, 0), at(1, 1, 0)
+    pc, px, py = at(0, 0, 1), at(0, 1, 0), at(1, 0, 0)
     half = kv.shape[0]
     rows = q_ref.shape[0]
+    tile = rows // 2
     z = lax.axis_index("tensor")
     mate = z + 1 - 2 * lax.rem(z, 2)
     outer = lax.rem(z, 3) == 0
@@ -67,10 +69,17 @@
         mine, theirs = head_cols(x, i), head_cols(1 - x, i)
         out = [send(q_ref.at[:, theirs], qx.at[i], first_q.at[i], rec_q.at[i], px)]
         for t, src in enumerate((ks_ref, vs_ref)):
-            out.append(send(src.at[:, theirs], kv.at[i, own, t], first_s.at[0, i, t], rec_kv.at[i, own], px))
-            out.append(send(src.at[:, mine], kv.at[i, own, t], first_s.at[1, i, t], rec_kv.at[i, own], py))
-            out.append(send(src.at[:, mine], kv.at[i, own, t], first_s.at[2, i, t], rec_kv.at[i, own], pc))
-            out.append(pltpu.make_async_copy(src.at[:, mine], kv.at[i, own, t], first_s.at[3, i, t]))
+            out.append(send(src.at[:, theirs], kv.at[i, t, PX], first_s.at[0, i, t], rec_kv.at[i, PX], px))
+            out.append(send(src.at[:, mine], kv.at[i, t, PY], first_s.at[1, i, t], rec_kv.at[i, PY], py))
+            out.append(send(src.at[:, mine], kv.at[i, t, PC], first_s.at[2, i, t], rec_kv.at[i, PC], pc))
+        return out
+
+    def locals_of(i):
+        mine = head_cols(x, i)
+        out = []
+        for t, (new, old) in enumerate(((kf_ref, ks_ref), (vf_ref, vs_ref))):
+            out.append(pltpu.make_async_copy(new.at[:, mine], kv.at[i, t, FRESH], first_s.at[3, i, t]))
+            out.append(pltpu.make_async_copy(old.at[:, mine], kv.at[i, t, OWN], first_s.at[4, i, t]))
         return out
 
     def weight_rows(core, i):
@@ -93,41 +102,54 @@
             weight_on(i, c).start()
 
     def start_first(i):
-        for copy in firsts(i):
+        for copy in firsts(i) + locals_of(i):
             copy.start()
 
         @pl.when(outer)
         def _():
             weight_out(i).start()
 
-    def fwd(kind, i, b, dev):
-        return send(kv.at[i, b], kv.at[i, b], fwd_s.at[kind, i], rec_kv.at[i, b], dev)
-
-    def arrived(i, b):
-        fwd(0, i, b, pc).wait_recv()
+    def fwd(kind, i):
+        slot, to, dev = ((PX, PYX, py), (PX, PXC, pc), (PY, PYC, pc), (PYX, PYXC, pc))[kind]
+        return send(kv.at[i, :, slot], kv.at[i, :, to], fwd_s.at[kind, i], rec_kv.at[i, to], dev)
+
+    def arrived(i, slot):
+        part = kv.at[i, :, slot]
+        send(part, part, fwd_s.at[0, i], rec_kv.at[i, slot], pc).wait_recv()
 
     def back(i):
         return (send(osend.at[i], orecv.at[i], ret_s.at[0, i], rec_o.at[0, i], px),
                 send(lsend.at[i], lrecv.at[i], ret_s.at[1, i], rec_o.at[1, i], px))
 
     def pass_on_x(i):
-        arrived(i, px)
-        fwd(0, i, px, py).start()
-        fwd(1, i, px, pc).start()
-
-    def fold(i, q, blocks):
-        for r in range(2):
-            m, acc = attend_block(q[r], kv[i, blocks[r], 0], kv[i, blocks[r], 1], m_s[r], acc_s[r])
-            m_s[r], acc_s[r] = m, acc
+        arrived(i, PX)
+        fwd(0, i).start()
+        fwd(1, i).start()
+
+    def query_tile(i, t):
+        if t < 2:
+            return q_ref[pl.ds(t * tile, tile), head_cols(x, i)]
+        return qx[i, pl.ds((t - 2) * tile, tile), :]
+
+    def keys_values(i, first, count):
+        return [kv[i, t, pl.ds(first, count)].reshape(count * rows, HD) for t in range(2)]
+
+    def start_state():
+        return jnp.full((tile, HD), -1e30, jnp.float32), jnp.zeros((tile, 2 * HD), jnp.float32)
+
+    def near(i, t, first, count):
+        m_s[t], acc_s[t] = attend_block(query_tile(i, t), *keys_values(i, first, count), *start_state())
 
     def merge(i):
         theirs = head_cols(1 - x, i)
         for copy in back(i):
             copy.wait_recv()
-        m = jnp.broadcast_to(lrecv[i][0:1, :], (HD, rows)).T[:, 0:1]
-        acc = jnp.concatenate([orecv[i].astype(jnp.float32), jnp.ones((rows, HD), jnp.float32)], axis=1)
-        m, acc = attend_block(q_ref[:, theirs], kf_ref[:, theirs], vf_ref[:, theirs], m, acc)
-        o_ref[:, theirs] = (acc[:, :HD] / acc[:, HD:]).astype(o_ref.dtype)
+        for t in range(2):
+            part = pl.ds(t * tile, tile)
+            m = jnp.broadcast_to(lrecv[i, 0:1, part], (HD, tile)).T
+            acc = jnp.concatenate([orecv[i, part, :].astype(jnp.float32), jnp.ones((tile, HD), jnp.float32)], axis=1)
+            m, acc = attend_block(q_ref[part, theirs], kf_ref[:, theirs], vf_ref[:, theirs], m, acc)
+            o_ref[part, theirs] = (acc[:, :HD] / acc[:, HD:]).astype(o_ref.dtype)
 
     barrier = pltpu.get_barrier_semaphore()
     for dev in (pc, px, py):
@@ -144,63 +166,51 @@
             start_first(i + 2)
 
         mine = head_cols(x, i)
-        m0 = jnp.full((rows, 1), -1e30, jnp.float32)
-        a0 = jnp.zeros((rows, 2 * HD), jnp.float32)
-        m_s[0], acc_s[0] = attend_block(q_ref[:, mine], kf_ref[:, mine], vf_ref[:, mine], m0, a0)
-        m_s[1], acc_s[1] = m0, a0
 
         @pl.when(i == 0)
         def _():
             pass_on_x(0)
 
-        send(q_ref.at[:, mine], qx.at[i], first_q.at[i], rec_q.at[i], px).wait_recv()
-        for t, src in enumerate((ks_ref, vs_ref)):
-            pltpu.make_async_copy(src.at[:, mine], kv.at[i, own, t], first_s.at[3, i, t]).wait()
-        arrived(i, pc)
-        arrived(i, at(0, 1, 1))
-
-        def queries():
-            return q_ref[:, mine], qx[i]
-
-        def near(t, _):
-            kx, kc = (t + 1) // 2, lax.rem(t + 1, 2)
-            b0 = at(0, kx, kc)
-            b1 = lax.rem(t, 2) * own + (1 - lax.rem(t, 2)) * b0
-            fold(i, queries(), (b0, b1))
-            return 0
-
-        lax.fori_loop(0, 3, near, 0)
+        for copy in locals_of(i):
+            copy.wait()
+        arrived(i, PC)
+        arrived(i, PXC)
+        for t in range(2):
+            near(i, t, FRESH, 4)
 
         @pl.when(i + 1 < half)
         def _():
             pass_on_x(i + 1)
 
-        arrived(i, py)
-        fwd(2, i, py, pc).start()
-        arrived(i, pyx)
-        fwd(3, i, pyx, pc).start()
-
-        def far(t, _):
-            @pl.when(t == 2)
-            def _():
-                arrived(i, at(1, 0, 1))
-                arrived(i, at(1, 1, 1))
-
-            b = at(1, lax.rem(t, 2), t // 2)
-            fold(i, queries(), (b, b))
-            return 0
-
-        lax.fori_loop(0, 4, far, 0)
-        o_ref[:, mine] = (acc_s[0][:, :HD] / acc_s[0][:, HD:]).astype(o_ref.dtype)
-        total = acc_s[1][:, HD:]
-        osend[i] = (acc_s[1][:, :HD] / total).astype(osend.dtype)
-        lsend[i] = (m_s[1] + jnp.log2(total)).T[0:8, :]
+        arrived(i, PY)
+        fwd(2, i).start()
+        arrived(i, PYX)
+        fwd(3, i).start()
+        firsts(i)[0].wait_recv()
+        for t in range(2, 4):
+            near(i, t, PC, 3)
+
+        @pl.when(i > 0)
+        def _():
+            merge(i - 1)
+
+        arrived(i, PYC)
+        arrived(i, PYXC)
+        for t in range(4):
+            m, acc = attend_block(query_tile(i, t), *keys_values(i, PY, 4), m_s[t], acc_s[t])
+            total = acc[:, HD:]
+            out = (acc[:, :HD] / total).astype(o_ref.dtype)
+            if t < 2:
+                o_ref[pl.ds(t * tile, tile), mine] = out
+            else:
+                part = pl.ds((t - 2) * tile, tile)
+                osend[i, part, :] = out
+                lsend[i, :, part] = (m + jnp.log2(total)).T[0:8, :]
         for copy in back(i):
             copy.start()
 
         @pl.when(i > 0)
         def _():
-            merge(i - 1)
             weight_pass(i - 1)
 
         return 0
@@ -223,9 +233,9 @@
         firsts_i[0].wait_send()
         for t in range(2):
             for k in range(3):
-                firsts_i[1 + 4 * t + k].wait_send()
-        for kind, (b, dev) in enumerate(((px, py), (px, pc), (py, pc), (pyx, pc))):
-            fwd(kind, i, b, dev).wait_send()
+                firsts_i[1 + 3 * t + k].wait_send()
+        for kind in range(4):
+            fwd(kind, i).wait_send()
         for copy in back(i):
             copy.wait_send()
         return 0
@@ -247,19 +257,19 @@
         out_shape=[jax.ShapeDtypeStruct((rows, cols), bf16),
                    jax.ShapeDtypeStruct((cols, out_weight.shape[1] // 2), bf16)],
         scratch_shapes=[
-            pltpu.VMEM((half, 8, 2, rows, HD), bf16),
+            pltpu.VMEM((half, 2, 9, rows, HD), bf16),
             pltpu.VMEM((half, rows, HD), bf16),
             pltpu.VMEM((half, rows, HD), bf16),
             pltpu.VMEM((half, rows, HD), bf16),
             pltpu.VMEM((half, 8, rows), f32),
             pltpu.VMEM((half, 8, rows), f32),
-            pltpu.VMEM((2, rows, 1), f32),
-            pltpu.VMEM((2, rows, 2 * HD), f32),
-            dma((4, half, 2)),
+            pltpu.VMEM((4, rows // 2, HD), f32),
+            pltpu.VMEM((4, rows // 2, 2 * HD), f32),
+            dma((5, half, 2)),
             dma((half,)),
             dma((4, half)),
             dma((2, half)),
-            dma((half, 8)),
+            dma((half, 9)),
             dma((half,)),
             dma((2, half)),
             dma((half,)),
@@ -329,7 +339,7 @@
 
     def store(r, total):
         o_ref[rows_of(r), :] = (
-            res_ref[rows_of(r), :].astype(jnp.float32) + gate_ref[...] * total
+            res_ref[rows_of(r), :].astype(jnp.float32) + gate_ref[...][None, :] * total
         ).astype(o_ref.dtype)
 
     barrier = pltpu.get_barrier_semaphore()
@@ -439,7 +449,7 @@
             collective_id=2, has_side_effects=True, vmem_limit_bytes=56 * 2**20
         ),
         name="line_project",
-    )(attended, out_weight, weight_mate, residual, gate[None, :])
+    )(attended, out_weight, weight_mate, residual, gate)
 
 
 def general_body(n, query, key_fresh, value_fresh, key_stale, value_stale, out_weight, residual, gate):

time: 174 us -> 160 us (0.920)
  Pallas kernels: 170 us -> 157 us
    pallas_call x1, Pallas kernels: 96.4 us -> 83.9 us  [paired_attention(): pl.pallas_call(attend_kernel, in_specs=[vmem, vmem, vmem, hbm, hbm, hbm],...]
where the time goes in v3:
time: 160 us
  Pallas kernels  157 us (98%)
  local copies, waits for them, and re-layouts  2.46 us (2%)
    pallas_call x1, Pallas kernels, paired_attention(): pl.pallas_call(attend_kernel, in_specs=[vmem, vmem, vmem, hbm, hbm, hbm],...  83.9 us
    pallas_call x1, Pallas kernels, line_project(): pl.pallas_call(project_kernel, in_specs=[vmem, hbm, hbm, vmem, vmem], out...  73.6 us

profile of v3, /device:TPU:8, one launch (start us, length us, event | category | flops | bytes accessed | tf_op | source)
XLA Modules:
  0.0 159.9 jit_solution(11957608274047730778)
XLA Ops:
  0.0 83.9 %paired_attention.1 = (bf16[512,1280]{1,0:T(8,128)(2,1)}, bf16[1280,2560]{1,0:T(8,128)(2,1)}) custom-call(bf16[512,1280]{1,0:T(8,128)(2,1)} %q_ref.1, bf16[512,1280]{1,0:T(8,128)(2,1)} %kf_ref.1, bf16[512,1280]{1,0:T(8,128)(2,1)} %vf_ref.1, bf16[512,1280]{1,0:T(8,128)(2,1)} %ks_ref.1, bf16[512,1280]{1,0:T(8,128)(2,1)} %vs_ref.1, bf16[1280,5120]{1,0:T(8,128)(2,1)} %w_ref.3), custom_call_target="tpu_custom_call" | custom-call | tf_op jit(solution)/shard_map/paired_attention/pallas_call | solution.py:253
  83.9 73.6 %line_project.1 = bf16[512,1280]{1,0:T(8,128)(2,1)} custom-call(bf16[512,1280]{1,0:T(8,128)(2,1)} %get-tuple-element.7.a_ref, bf16[1280,5120]{1,0:T(8,128)(2,1)} %w_ref.3, bf16[1280,2560]{1,0:T(8,128)(2,1)} %get-tuple-element.8.wx_ref, bf16[512,1280]{1,0:T(8,128)(2,1)} %res_ref.1, f32[1280]{0:T(1024)} %gate_ref.1), custom_call_target="tpu_custom_call" | custom-call | tf_op jit(solution)/shard_map/line_project/pallas_call | solution.py:432
  157.5 2.5 %copy.10 = bf16[512,1280]{1,0:T(8,128)(2,1)} copy(bf16[512,1280]{1,0:T(8,128)(2,1)} %line_project.1) | data formatting | bytes 2621440

commit v4 on v3

--- a/solution.py
+++ b/solution.py
@@ -105,6 +105,7 @@
         for copy in firsts(i) + locals_of(i):
             copy.start()
 
+    def start_weight(i):
         @pl.when(outer)
         def _():
             weight_out(i).start()
@@ -158,18 +159,20 @@
     pl.semaphore_wait(barrier, 4)
 
     start_first(0)
-    start_first(1)
+    start_weight(0)
 
     def one_head(i, _):
-        @pl.when(i + 2 < half)
-        def _():
-            start_first(i + 2)
+        @pl.when(i + 1 < half)
+        def _():
+            start_weight(i + 1)
 
         mine = head_cols(x, i)
 
         @pl.when(i == 0)
         def _():
             pass_on_x(0)
+            if half > 1:
+                start_first(1)
 
         for copy in locals_of(i):
             copy.wait()
@@ -181,6 +184,10 @@
         @pl.when(i + 1 < half)
         def _():
             pass_on_x(i + 1)
+
+        @pl.when(i + 2 < half)
+        def _():
+            start_first(i + 2)
 
         arrived(i, PY)
         fwd(2, i).start()
@@ -209,13 +216,15 @@
         for copy in back(i):
             copy.start()
 
-        @pl.when(i > 0)
-        def _():
-            weight_pass(i - 1)
+        @pl.when(i > 1)
+        def _():
+            weight_pass(i - 2)
 
         return 0
 
     lax.fori_loop(0, half, one_head, 0)
+    for i in range(max(half - 2, 0), half - 1):
+        weight_pass(i)
     merge(half - 1)
     weight_pass(half - 1)
 

time: 160 us -> 156 us (0.975)
  Pallas kernels: 157 us -> 153 us
    pallas_call x1, Pallas kernels: 83.9 us -> 80.7 us  [paired_attention(): pl.pallas_call(attend_kernel, in_specs=[vmem, vmem, vmem, hbm, hbm, hbm],...]
where the time goes in v4:
time: 156 us
  Pallas kernels  153 us (98%)
  local copies, waits for them, and re-layouts  2.46 us (2%)
    pallas_call x1, Pallas kernels, paired_attention(): pl.pallas_call(attend_kernel, in_specs=[vmem, vmem, vmem, hbm, hbm, hbm],...  80.7 us
    pallas_call x1, Pallas kernels, line_project(): pl.pallas_call(project_kernel, in_specs=[vmem, hbm, hbm, vmem, vmem], out...  72.8 us

profile of v4, /device:TPU:8, one launch (start us, length us, event | category | flops | bytes accessed | tf_op | source)
XLA Modules:
  0.0 156.0 jit_solution(6754363808257729516)
XLA Ops:
  0.0 80.7 %paired_attention.1 = (bf16[512,1280]{1,0:T(8,128)(2,1)}, bf16[1280,2560]{1,0:T(8,128)(2,1)}) custom-call(bf16[512,1280]{1,0:T(8,128)(2,1)} %q_ref.1, bf16[512,1280]{1,0:T(8,128)(2,1)} %kf_ref.1, bf16[512,1280]{1,0:T(8,128)(2,1)} %vf_ref.1, bf16[512,1280]{1,0:T(8,128)(2,1)} %ks_ref.1, bf16[512,1280]{1,0:T(8,128)(2,1)} %vs_ref.1, bf16[1280,5120]{1,0:T(8,128)(2,1)} %w_ref.3), custom_call_target="tpu_custom_call" | custom-call | tf_op jit(solution)/shard_map/paired_attention/pallas_call | solution.py:262
  80.7 72.8 %line_project.1 = bf16[512,1280]{1,0:T(8,128)(2,1)} custom-call(bf16[512,1280]{1,0:T(8,128)(2,1)} %get-tuple-element.7.a_ref, bf16[1280,5120]{1,0:T(8,128)(2,1)} %w_ref.3, bf16[1280,2560]{1,0:T(8,128)(2,1)} %get-tuple-element.8.wx_ref, bf16[512,1280]{1,0:T(8,128)(2,1)} %res_ref.1, f32[1280]{0:T(1024)} %gate_ref.1), custom_call_target="tpu_custom_call" | custom-call | tf_op jit(solution)/shard_map/line_project/pallas_call | solution.py:441
  153.5 2.5 %copy.10 = bf16[512,1280]{1,0:T(8,128)(2,1)} copy(bf16[512,1280]{1,0:T(8,128)(2,1)} %line_project.1) | data formatting | bytes 2621440
